TPU v7x, 512 devices: a whole 4x4x16 slice. The times are simulated.
512 devices in a mesh: line: 8 (over x, core), surf: 64 (over z, y).
Axes of the slice: x: 4, y: 4, z: 16, core: 2. Of those that a mesh axis runs over, the one named last changes fastest.
Arguments:
- residual: float32 [64, 13, 16384], P('line', None, 'surf'), may hold values from -0.6 to 0.6
- previous: float32 [64, 13, 16384], P('line', None, 'surf'), may hold values from -6 to 6
- edge_blocks: bfloat16 [64, 13, 13, 16384], P('line', None, None, 'surf'), as said below
- damping: float32 [64, 13, 16384], P('line', None, 'surf'), may hold values from 0.004 to 0.016
- lateral: float32 [64, 4, 16384], P('line', None, 'surf'), may hold values from 0.004 to 0.04
- coupling: float32 [13, 13], replicated, may hold values from -1.75 to 1.75
- wall_flags: int32 [16384], P('surf'), may hold values 0 or 1
- wall_gain: float32 [13], replicated, may hold values from 0.5 to 4
- face_table: int32 [64, 4, 2], P('surf'), may hold values from 0 to 63, as said below
Outputs:
- updated: float32 [64, 13, 16384], P('line', None, 'surf')
Inputs may be any that keep to these rules, and one draw needn't show every extreme that they name: Each edge_blocks[i, :, :, s] is symmetric, and each of its diagonal entries exceeds the sum of magnitudes of the other entries of its row by more than 0.25. `face_table`: entry [p, f] is (q, r): face f of patch p meets face f xor 1 of patch q, positions mirrored if r is 1; the relation is symmetric with the same r on both sides; the four peers of a patch are four different patches, none the patch itself.
All inputs are finite; a program needn't handle non-finite values. No bound on the sum of `wall_flags` on one device may be relied on, other than what follows from the above.
Results may differ from a plain program's by a relative error of at most 0.0003.
Values sent between devices are 32-bit elements; how exact they have to be, the bound alone decides.
A program may use at most 128 MiB of HBM per device.

v0:
```python
import jax
import jax.numpy as jnp
from jax import lax
from jax.sharding import PartitionSpec as P

NSPEC = 13
PW = 16


def product(left_mat, right_mat):
    return jnp.sum(left_mat[:, :, None, :] * right_mat[None, :, :, :], axis=1)


def product_vec(matrix, vector):
    return jnp.sum(matrix * vector[None, :, :], axis=1)


def transposed(left_mat, right_mat):
    return jnp.sum(left_mat[:, :, None, :] * right_mat[:, None, :, :], axis=0)


def transposed_vec(matrix, vector):
    return jnp.sum(matrix * vector[:, None, :], axis=0)


def invert(matrix):
    order_size = matrix.shape[0]
    inverse = jnp.broadcast_to(jnp.eye(order_size, dtype=jnp.float32)[:, :, None], matrix.shape)
    for pivot_at in range(order_size):
        reciprocal = 1.0 / matrix[pivot_at, pivot_at]
        row_mat = matrix[pivot_at] * reciprocal
        row_inv = inverse[pivot_at] * reciprocal
        column = matrix[:, pivot_at]
        matrix = (matrix - column[:, None] * row_mat[None]).at[pivot_at].set(row_mat)
        inverse = (inverse - column[:, None] * row_inv[None]).at[pivot_at].set(row_inv)
    return inverse


def factor_step(carried, stored):
    diagonal, lower_here, upper_here = stored
    inverse = invert(diagonal - product(lower_here, carried))
    gain_here = product(inverse, upper_here)
    return (gain_here, (inverse, gain_here))


def interior_solve(inverses, lowers, gain_all, sources):

    def forward(carried, stored):
        inverse, lower_here, source = stored
        partial_value = product(inverse, source + product(lower_here, carried))
        return (partial_value, partial_value)

    _, partials = lax.scan(forward, jnp.zeros_like(sources[0]), (inverses, lowers, sources))

    def interior_backward(carried, stored):
        gain_here, partial_value = stored
        solved = partial_value + product(gain_here, carried)
        return (solved, solved)

    _, solved = lax.scan(
        interior_backward, jnp.zeros_like(sources[0]), (gain_all, partials), reverse=True
    )
    return solved


def reduced_factor(diagonals, uppers):

    def forward(carried, stored):
        diagonal, upper_here = stored
        inverse = invert(diagonal - carried)
        gain_here = product(inverse, upper_here)
        return (transposed(upper_here, gain_here), (inverse, gain_here))

    _, (inverses, gain_all) = lax.scan(forward, jnp.zeros_like(diagonals[0]), (diagonals, uppers))
    return (inverses, gain_all)


def reduced_solve(inverses, gain_all, uppers, sources):

    def forward(carried, stored):
        inverse, upper_here, source = stored
        partial_value = product_vec(inverse, source - carried)
        return (transposed_vec(upper_here, partial_value), partial_value)

    _, partials = lax.scan(forward, jnp.zeros_like(sources[0]), (inverses, uppers, sources))

    def reduced_backward(carried, stored):
        gain_here, partial_value = stored
        solved = partial_value - product_vec(gain_here, carried)
        return (solved, solved)

    _, solved = lax.scan(
        reduced_backward, jnp.zeros_like(sources[0]), (gain_all, partials), reverse=True
    )
    return solved


def spread_cells(spikes, values):
    return jnp.sum(spikes * values[None, None, :, :], axis=2)


def ghost_term(update, face_table, lateral, coupling):
    segment = update.shape[0]
    line_count = update.shape[2]
    patch_side = PW
    line_grid = update.reshape(segment, NSPEC, patch_side, patch_side)
    own_faces = jnp.stack(
        [
            line_grid[:, :, 0, :],
            line_grid[:, :, patch_side - 1, :],
            line_grid[:, :, :, 0],
            line_grid[:, :, :, patch_side - 1],
        ]
    )
    own_faces = own_faces.reshape(4, segment * NSPEC * patch_side)
    peers = face_table[0, :, 0]
    all_faces = lax.all_gather(own_faces, "surf", axis=0, tiled=True)
    partner = peers * 4 + jnp.array([1, 0, 3, 2], dtype=jnp.int32)
    ghosts = jnp.take(all_faces, partner, axis=0).reshape(4, segment, NSPEC, patch_side)
    ghosts = jnp.where(face_table[0, :, 1][:, None, None, None] == 1, ghosts[:, :, :, ::-1], ghosts)
    column = jnp.arange(line_count, dtype=jnp.int32) % patch_side
    zero_line = jnp.zeros_like(update[:, :, :1])
    lower_row = jnp.concatenate([ghosts[0], update[:, :, : line_count - patch_side]], axis=2)
    upper_row = jnp.concatenate([update[:, :, patch_side:], ghosts[1]], axis=2)
    lower_col = jnp.where(
        column == 0,
        jnp.repeat(ghosts[2], patch_side, axis=2),
        jnp.concatenate([zero_line, update[:, :, :-1]], axis=2),
    )
    upper_col = jnp.where(
        column == patch_side - 1,
        jnp.repeat(ghosts[3], patch_side, axis=2),
        jnp.concatenate([update[:, :, 1:], zero_line], axis=2),
    )
    weighted = lateral[:, 0, None, :] * lower_row + lateral[:, 1, None, :] * upper_row
    weighted = weighted + lateral[:, 2, None, :] * lower_col + lateral[:, 3, None, :] * upper_col
    return jnp.sum(coupling[None, :, :, None] * weighted[:, None, :, :], axis=2)


def segment_lines(edge_full, damping, wall_flags, wall_gain):
    segment = edge_full.shape[0]
    line_place = lax.axis_index("line")
    identity = jnp.eye(NSPEC, dtype=jnp.float32)[:, :, None]
    wall_diag = (
        wall_gain[:, None]
        * wall_flags.astype(jnp.float32)[None, :]
        * (line_place == 0).astype(jnp.float32)
    )
    diag_extra = damping[: segment - 1].at[0].add(wall_diag)
    diagonals = (
        edge_full[: segment - 1] + edge_full[1:] + identity[None] * diag_extra[:, None, :, :]
    )
    lowers = jnp.concatenate([jnp.zeros_like(edge_full[:1]), edge_full[1 : segment - 1]], axis=0)
    _, (inverses, gain_all) = lax.scan(
        factor_step, jnp.zeros_like(edge_full[0]), (diagonals, lowers, edge_full[1:])
    )
    left_edge = edge_full[0] * (line_place > 0).astype(jnp.float32)
    right_edge = edge_full[segment - 1]
    zero_block = jnp.zeros_like(edge_full[: segment - 1])
    columns = jnp.concatenate(
        [zero_block.at[0].set(left_edge), zero_block.at[segment - 2].set(right_edge)], axis=2
    )
    spikes = interior_solve(inverses, lowers, gain_all, columns)
    from_left = spikes[:, :, :NSPEC]
    from_right = spikes[:, :, NSPEC:]
    push_block = left_edge - product(left_edge, from_left[0])
    cross_block = product(left_edge, from_right[0])
    own_block = (
        right_edge
        + identity * damping[segment - 1][None]
        - product(right_edge, from_right[segment - 2])
    )
    all_own, all_push, all_cross = (
        lax.all_gather(own_block[None], "line", axis=0, tiled=True),
        lax.all_gather(push_block[None], "line", axis=0, tiled=True),
        lax.all_gather(cross_block[None], "line", axis=0, tiled=True),
    )
    all_pivots = all_own + jnp.concatenate([all_push[1:], jnp.zeros_like(all_push[:1])], axis=0)
    all_uppers = -jnp.concatenate([all_cross[1:], jnp.zeros_like(all_cross[:1])], axis=0)
    all_inverses, all_gains = reduced_factor(all_pivots, all_uppers)

    def sweep(source):
        interior = interior_solve(inverses, lowers, gain_all, source[: segment - 1, :, None, :])[
            :, :, 0, :
        ]
        own_source = source[segment - 1] + product_vec(right_edge, interior[segment - 2])
        tip_term = product_vec(left_edge, interior[0])
        all_base, all_tips = (
            lax.all_gather(own_source[None], "line", axis=0, tiled=True),
            lax.all_gather(tip_term[None], "line", axis=0, tiled=True),
        )
        all_sources = all_base + jnp.concatenate(
            [all_tips[1:], jnp.zeros_like(all_tips[:1])], axis=0
        )
        solved = reduced_solve(all_inverses, all_gains, all_uppers, all_sources)
        separator = lax.dynamic_index_in_dim(solved, line_place, 0, keepdims=False)
        lower_value = lax.dynamic_index_in_dim(
            solved, jnp.maximum(line_place - 1, 0), 0, keepdims=False
        )
        lower_value = lower_value * (line_place > 0).astype(jnp.float32)
        interior_full = interior + spread_cells(from_left, lower_value)
        interior_full = interior_full + spread_cells(from_right, separator)
        return jnp.concatenate([interior_full, separator[None]], axis=0)

    return sweep


def body(
    residual, previous, edge_blocks, damping, lateral, coupling, wall_flags, wall_gain, face_table
):
    edge_full = edge_blocks.astype(jnp.float32)
    sweep = segment_lines(edge_full, damping, wall_flags, wall_gain)
    sweep_one = sweep(residual - ghost_term(previous, face_table, lateral, coupling))
    return sweep(residual - ghost_term(sweep_one, face_table, lateral, coupling))


def solution(mesh):
    placed = (
        P("line", None, "surf"),
        P("line", None, "surf"),
        P("line", None, None, "surf"),
        P("line", None, "surf"),
        P("line", None, "surf"),
        P(),
        P("surf"),
        P(),
        P("surf", None, None),
    )
    return jax.shard_map(
        body, mesh=mesh, in_specs=placed, out_specs=P("line", None, "surf"), check_vma=False
    )
```

profile of v0, /device:TPU:1, one launch (start us, length us, event | category | flops | bytes accessed | tf_op | source)
XLA Modules:
  0.0 703.6 jit_solution(9495001896778752222)
XLA Ops:
  7.4 1.2 reshape.2987
  12.7 1.3 copy_convert_fusion
  14.1 2.1 fusion.138
  16.3 1.4 concatenate.204
  17.6 42.6 %while.232 = (s32[]{:T(128)}, f32[13,13,256]{2,1,0:T(8,128)S(1)}, f32[7,13,13,256]{3,2,1,0:T(8,128)}, f32[7,13,13,256]{3,2,1,0:T(8,128)}, f32[7,13,13,256]{3,2,1...) while((s32[]{:T(128)}, f32[13,13,256]{2,1,0:T(8,128)S(1)}, ...), condition=%wide.region_3.0_spmd, body=%wide.region_0.3_spmd.sunk | while | flops 4539771 | bytes 14211601 | solution.py:154
  62.2 86.5 %all-gather.19.cloned.1.call-done = f32[64,4,1664]{2,1,0:T(4,128)} async-done(((f32[1,4,1664]{2,1,0:T(4,128)}), f32[64,4,1664]{2,1,0:T(4,128)}) %all-gather.19.cloned.1.call-update) | async-done | bytes 1703952 | tf_op jit(solution)/shard_map/all_gather | solution.py:117
  148.7 2.8 reshape.3024
  151.6 2.0 gather_fusion
  157.3 1.2 fusion.127
  159.6 14.4 %while.233 = (s32[]{:T(128)}, f32[13,1,256]{2,0,1:T(8,128)S(1)}, f32[7,13,1,256]{3,2,1,0:T(1,128)S(1)}, f32[7,13,13,256]{3,2,1,0:T(8,128)}, f32[7,13,1,256]{3,0,...) while((s32[]{:T(128)}, f32[13,1,256]{2,0,1:T(8,128)S(1)}, f32[7,13,1,256]{3,2,1,0:T(1,128)S(1)}, ...), condition=%wide.region_8.10_spmd, body=%wide.region_5.9_spmd.sunk | while | flops 169730 | bytes 495709 | solution.py:53
  174.0 7.6 %while.239 = (s32[]{:T(128)}, f32[13,1,256]{2,1,0:T(1,128)S(1)}, f32[7,13,1,256]{3,1,2,0:T(8,128)S(1)}, f32[7,13,1,256]{3,2,1,0:T(1,128)S(1)}, f32[7,13,13,256]{...) while((s32[]{:T(128)}, f32[13,1,256]{2,1,0:T(1,128)S(1)}, ...), condition=%wide.region_11.13_spmd.clone, body=%wide.region_9.12_spmd.clone.sunk | while | flops 93188 | bytes 352375 | solution.py:60
  182.3 1.9 select_maximum_fusion
  184.3 2.0 broadcast.2023.clone
  186.3 27.4 %while.234 = (s32[]{:T(128)}, f32[13,26,256]{2,1,0:T(8,128)S(1)}, f32[7,13,26,256]{3,2,1,0:T(8,128)}, f32[7,13,13,256]{3,2,1,0:T(8,128)}, f32[7,13,26,256]{3,2,1...) while((s32[]{:T(128)}, f32[13,26,256]{2,1,0:T(8,128)S(1)}, f32[7,13,26,256]{3,2,1,0:T(8,128)}, ...), condition=%wide.region_15.17_spmd, body=%wide.region_12.16_spmd.sunk | while | flops 4412930 | bytes 4233813 | solution.py:53
  214.1 37.0 %while.240 = (s32[]{:T(128)}, f32[13,26,256]{2,1,0:T(8,128)}, f32[7,13,26,256]{3,2,1,0:T(8,128)S(1)}, f32[7,13,26,256]{3,2,1,0:T(8,128)}, f32[7,13,13,256]{3,2,1,0:T(8,128)}, /*index=5*/s32[]{:T(128)}, s32[]{:T(128)}, s32[]{:T(128)}) while((s32[]{:T(128)}, f32[13,26,256]{2,1,0:T(8,128)}, f32[7,13,26,256]{3,2,1,0:T(8,128)S(1)}, ...), condition=%wide.region_18.20_spmd.clone, body=%wide.region_16.19_spmd.clone.sunk | while | flops 2422788 | bytes 4140151 | solution.py:60
  215.6 1.1 fusion.292
  216.7 1.9 bitcast_add_fusion.11
  221.1 1.1 fusion.292
  222.1 1.9 bitcast_add_fusion.11
  226.5 1.1 fusion.292
  227.6 1.9 bitcast_add_fusion.11
  231.9 1.1 fusion.292
  233.0 1.9 bitcast_add_fusion.11
  237.3 1.1 fusion.292
  238.4 1.9 bitcast_add_fusion.11
  242.8 1.1 fusion.292
  243.8 1.9 bitcast_add_fusion.11
  248.2 1.1 fusion.292
  249.3 1.9 bitcast_add_fusion.11
  251.2 1.1 multiply_reduce_fusion.7
  254.6 1.2 multiply_reduce_fusion.8
  255.8 1.7 bitcast_subtract_fusion.9
  258.5 23.0 %all-gather.4 = f32[8,13,256]{2,1,0:T(8,128)S(1)} all-gather(f32[1,13,256]{2,1,0:T(8,128)} %bitcast.802), channel_id=3, replica_groups=mesh['line'=8,'surf'=64] {'line'}, dimensions={0}, use_global_device_ids=true | all-gather | bytes 119808 | tf_op jit(solution)/shard_map/all_gather | solution.py:190
  281.6 12.8 %all_gather.31 = f32[8,13,256]{2,1,0:T(8,128)S(1)} all-gather(f32[1,13,256]{2,1,0:T(8,128)S(1)} %copy.206), channel_id=1, replica_groups=mesh['line'=8,'surf'=64] {'line'}, dimensions={0}, use_global_device_ids=true | all-gather | bytes 119808 | tf_op jit(solution)/shard_map/all_gather | solution.py:189
  295.0 2.6 slice.2250
  297.6 27.9 %all-gather.17.cloned.1.call-done = f32[104,13,256]{2,1,0:T(8,128)} async-done(((f32[13,13,256]{2,1,0:T(8,128)}), f32[104,13,256]{2,1,0:T(8,128)}) %all-gather.17.cloned.1.call-update) | async-done | bytes 1384464 | tf_op jit(solution)/shard_map/all_gather | solution.py:176
  325.6 1.4 slice-done
  326.9 1.4 pad_negate_fusion
  328.4 31.7 %all-gather.13.cloned.1.call-done = f32[8,13,13,256]{3,2,1,0:T(8,128)} async-done(((f32[1,13,13,256]{3,2,1,0:T(8,128)}), f32[8,13,13,256]{3,2,1,0:T(8,128)}) %all-gather.13.cloned.1.call-update) | async-done | bytes 1384464 | tf_op jit(solution)/shard_map/all_gather | solution.py:174
  360.1 3.5 pad_add_fusion
  363.6 40.8 %while.235 = (s32[]{:T(128)}, f32[13,13,256]{2,1,0:T(8,128)S(1)}, f32[8,13,13,256]{3,2,1,0:T(8,128)}, f32[8,13,13,256]{3,2,1,0:T(8,128)}, f32[8,13,13,256]{3,2,1...) while((s32[]{:T(128)}, f32[13,13,256]{2,1,0:T(8,128)S(1)}, f32[8,13,13,256]{3,2,1,0:T(8,128)}, ...), condition=%wide.region_25.27_spmd, body=%wide.region_22.26_spmd.sunk | while | flops 4539771 | bytes 13865477 | solution.py:74
  404.4 21.7 %while.236 = (s32[]{:T(128)}, f32[13,256]{1,0:T(8,128)S(1)}, f32[8,13,256]{2,1,0:T(8,128)S(1)}, f32[8,13,13,256]{3,2,1,0:T(8,128)}, f32[8,13,13,256]{3,2,1,0:T(8,128)}, /*index=5*/f32[8,13,256]{2,1,0:T(8,128)}, s32[]{:T(128)}) while((s32[]{:T(128)}, f32[13,256]{1,0:T(8,128)S(1)}, f32[8,13,256]{2,1,0:T(8,128)S(1)}, ...), condition=%wide.region_31.33_spmd, body=%wide.region_28.32_spmd.sunk | while | flops 169730 | bytes 472157 | solution.py:85
  426.7 12.9 %while.241 = (s32[]{:T(128)}, f32[13,256]{1,0:T(8,128)S(1)}, f32[8,13,256]{2,1,0:T(8,128)}, f32[8,13,256]{2,1,0:T(8,128)S(1)}, f32[8,13,13,256]{3,2,1,0:T(8,128)}, /*index=5*/s32[]{:T(128)}, s32[]{:T(128)}, s32[]{:T(128)}) while((s32[]{:T(128)}, f32[13,256]{1,0:T(8,128)S(1)}, f32[8,13,256]{2,1,0:T(8,128)}, ...), condition=%wide.region_34.36_spmd.clone, body=%wide.region_32.35_spmd.clone.sunk | while | flops 93188 | bytes 309367 | solution.py:92
  441.2 1.2 reshape.2991
  442.4 2.9 fusion.140
  445.3 1.2 fusion.139
  446.6 2.0 copy.211
  448.6 2.0 copy.212
  453.1 129.8 %all-gather.21.cloned.1.call-done = f32[64,4,1664]{2,1,0:T(4,128)} async-done(((f32[1,4,1664]{2,1,0:T(4,128)}), f32[64,4,1664]{2,1,0:T(4,128)}) %all-gather.21.cloned.1.call-update) | async-done | bytes 1703952 | tf_op jit(solution)/shard_map/all_gather | solution.py:117
  583.0 2.8 reshape.3028
  585.8 2.2 gather_fusion.1
  588.9 1.8 rev.7
  590.6 1.1 broadcast_select_fusion.5
  592.5 1.2 broadcast_in_dim.282
  593.7 2.1 reshape.2993
  596.7 1.2 broadcast_in_dim.288
  597.9 2.1 reshape.2994
  600.1 1.3 fusion.130
  603.4 18.4 %while.237 = (s32[]{:T(128)}, f32[13,1,256]{2,0,1:T(8,128)S(1)}, f32[7,13,1,256]{3,2,1,0:T(1,128)}, f32[7,13,13,256]{3,2,1,0:T(8,128)}, f32[7,13,1,256]{3,0,1,2:...) while((s32[]{:T(128)}, f32[13,1,256]{2,0,1:T(8,128)S(1)}, f32[7,13,1,256]{3,2,1,0:T(1,128)}, ...), condition=%wide.region_41.43_spmd, body=%wide.region_38.42_spmd.sunk | while | flops 169730 | bytes 493145 | solution.py:53
  621.7 12.6 %while.242 = (s32[]{:T(128)}, f32[13,1,256]{2,1,0:T(1,128)S(1)}, f32[7,13,1,256]{3,1,2,0:T(8,128)S(1)}, f32[7,13,1,256]{3,2,1,0:T(1,128)}, f32[7,13,13,256]{3,2,1,0:T(8,128)}, /*index=5*/s32[]{:T(128)}, s32[]{:T(128)}, s32[]{:T(128)}) while((s32[]{:T(128)}, f32[13,1,256]{2,1,0:T(1,128)S(1)}, f32[7,13,1,256]{3,1,2,0:T(8,128)S(1)}, ...), condition=%wide.region_44.46_spmd.clone, body=%wide.region_42.45_spmd.clone.sunk | while | flops 93188 | bytes 352375 | solution.py:60
  634.4 22.7 %all-gather.6 = f32[8,13,256]{2,1,0:T(8,128)S(1)} all-gather(f32[1,13,256]{2,1,0:T(8,128)S(1)} %bitcast.803), channel_id=4, replica_groups=mesh['line'=8,'surf'=64] {'line'}, dimensions={0}, use_global_device_ids=true | all-gather | bytes 119808 | tf_op jit(solution)/shard_map/all_gather | solution.py:190
  658.1 12.8 %all_gather.34 = f32[8,13,256]{2,1,0:T(8,128)S(1)} all-gather(f32[1,13,256]{2,1,0:T(8,128)S(1)} %copy.221), channel_id=1, replica_groups=mesh['line'=8,'surf'=64] {'line'}, dimensions={0}, use_global_device_ids=true | all-gather | bytes 119808 | tf_op jit(solution)/shard_map/all_gather | solution.py:189
  670.9 16.0 %while.238 = (s32[]{:T(128)}, f32[13,256]{1,0:T(8,128)S(1)}, f32[8,13,256]{2,1,0:T(8,128)S(1)}, f32[8,13,13,256]{3,2,1,0:T(8,128)}, f32[8,13,13,256]{3,2,1,0:T(8,128)}, /*index=5*/f32[8,13,256]{2,1,0:T(8,128)S(1)}, s32[]{:T(128)}) while((s32[]{:T(128)}, f32[13,256]{1,0:T(8,128)S(1)}, f32[8,13,256]{2,1,0:T(8,128)S(1)}, ...), condition=%wide.region_50.52_spmd, body=%wide.region_47.51_spmd.sunk | while | flops 169730 | bytes 472157 | solution.py:85
  687.0 8.5 %while.243 = (s32[]{:T(128)}, f32[13,256]{1,0:T(8,128)S(1)}, f32[8,13,256]{2,1,0:T(8,128)S(1)}, f32[8,13,256]{2,1,0:T(8,128)S(1)}, f32[8,13,13,256]{3,2,1,0:T(8,128)}, /*index=5*/s32[]{:T(128)}, s32[]{:T(128)}, s32[]{:T(128)}) while((s32[]{:T(128)}, f32[13,256]{1,0:T(8,128)S(1)}, f32[8,13,256]{2,1,0:T(8,128)S(1)}, ...), condition=%wide.region_53.55_spmd.clone, body=%wide.region_51.54_spmd.clone.sunk | while | flops 93188 | bytes 315511 | solution.py:92
  (1809 shorter events, 256.2 us)
Async XLA Ops:
  6.5 142.2 %all-gather.19.cloned.1.call-start = ((), (), s32[]{:S(2)}) async-start(), calls=%async_computation.3 | async-start | bytes 1730560 | tf_op jit(solution)/shard_map/all_gather | solution.py:117
  8.9 3.6 copy-start.25
  8.9 3.6 copy-start.26
  11.8 283.2 %all-gather.15.cloned.1.call-start = ((), (), s32[]{:S(2)}) async-start(), calls=%async_computation.1 | async-start | bytes 1916928 | tf_op jit(solution)/shard_map/all_gather | solution.py:175
  14.0 167.6 %copy-start = (f32[8,13,13,256]{3,2,1,0:T(8,128)}, f32[8,13,13,256]{3,2,1,0:T(8,128)S(1)}, u32[]{:S(2)}) copy-start(f32[8,13,13,256]{3,2,1,0:T(8,128)S(1)} %copy_convert_fusion) | copy-start | bytes 4153348
  17.6 42.7 %copy-start.1 = (f32[8,13,256]{2,0,1:T(8,128)S(1)}, f32[8,13,256]{2,0,1:T(8,128)}, u32[]{:S(2)}) copy-start(f32[8,13,256]{2,0,1:T(8,128)} %param.144) | copy-start | bytes 319492
  60.3 1.0 copy-start.27
  60.3 1.0 copy-start.28
  60.3 1.1 copy-start.15
  61.3 92.3 %copy-start.17 = (pred[4]{0:T(512)(128)(4,1)}, pred[4]{0:T(512)(128)(4,1)S(1)}, u32[]{:S(2)}) copy-start(pred[4]{0:T(512)(128)(4,1)S(1)} %get-tuple-element.1995) | copy-start | bytes 16
  61.3 90.3 %copy-start.16 = (s32[1024]{0:T(1024)}, s32[1024]{0:T(1024)S(1)}, u32[]{:S(2)}) copy-start(s32[1024]{0:T(1024)S(1)} %pad_clamp_fusion) | copy-start | bytes 12292
  61.3 92.6 %copy-start.23 = (pred[4]{0:T(512)(128)(4,1)}, pred[4]{0:T(512)(128)(4,1)S(1)}, u32[]{:S(2)}) copy-start(pred[4]{0:T(512)(128)(4,1)S(1)} %compare_bitcast_fusion) | copy-start | bytes 16
  61.4 95.9 %copy-start.5 = (f32[8,256]{1,0:T(8,128)}, f32[8,256]{1,0:T(8,128)S(1)}, u32[]{:S(2)}) copy-start(f32[8,256]{1,0:T(8,128)S(1)} %get-tuple-element.2191) | copy-start | bytes 24580
  61.4 95.9 %copy-start.7 = (f32[8,256]{1,0:T(8,128)}, f32[8,256]{1,0:T(8,128)S(1)}, u32[]{:S(2)}) copy-start(f32[8,256]{1,0:T(8,128)S(1)} %get-tuple-element.2192) | copy-start | bytes 24580
  61.4 95.9 %copy-start.9 = (f32[8,256]{1,0:T(8,128)}, f32[8,256]{1,0:T(8,128)S(1)}, u32[]{:S(2)}) copy-start(f32[8,256]{1,0:T(8,128)S(1)} %get-tuple-element.2193) | copy-start | bytes 24580
  61.4 95.9 %copy-start.11 = (f32[8,256]{1,0:T(8,128)}, f32[8,256]{1,0:T(8,128)S(1)}, u32[]{:S(2)}) copy-start(f32[8,256]{1,0:T(8,128)S(1)} %get-tuple-element.2194) | copy-start | bytes 24580
  155.0 2.3 copy-start.19
  155.0 2.3 copy-start.21
  156.0 2.6 copy-start.13
  156.0 2.8 copy-start.4
  158.9 0.6 copy-start.3
  253.1 72.5 %all-gather.17.cloned.1.call-start = ((), (), s32[]{:S(2)}) async-start(), calls=%async_computation.2 | async-start | bytes 1916928 | tf_op jit(solution)/shard_map/all_gather | solution.py:176
  253.8 106.3 %all-gather.13.cloned.1.call-start = ((), (), s32[]{:S(2)}) async-start(), calls=%async_computation | async-start | bytes 1916928 | tf_op jit(solution)/shard_map/all_gather | solution.py:174
  257.5 325.5 %all-gather.21.cloned.1.call-start = ((), (), s32[]{:S(2)}) async-start(), calls=%async_computation.4 | async-start | bytes 1730560 | tf_op jit(solution)/shard_map/all_gather | solution.py:117
  325.6 1.4 slice-start
  453.1 134.8 %copy-start.18 = (pred[4]{0:T(512)(128)(4,1)S(1)}, pred[4]{0:T(512)(128)(4,1)}, u32[]{:S(2)}) copy-start(pred[4]{0:T(512)(128)(4,1)} %copy-done.17) | copy-start | bytes 16
  453.1 137.5 %copy-start.24 = (pred[4]{0:T(512)(128)(4,1)S(1)}, pred[4]{0:T(512)(128)(4,1)}, u32[]{:S(2)}) copy-start(pred[4]{0:T(512)(128)(4,1)} %copy-done.23) | copy-start | bytes 16
  592.4 7.6 %copy-start.2 = (f32[8,13,255]{2,1,0:T(8,128)S(1)}, f32[8,13,255]{2,1,0:T(8,128)}, u32[]{:S(2)}) copy-start(f32[8,13,255]{2,1,0:T(8,128)} %get-tuple-element.2170) | copy-start | bytes 318244
  592.5 7.6 %copy-start.6 = (f32[8,256]{1,0:T(8,128)S(1)}, f32[8,256]{1,0:T(8,128)}, u32[]{:S(2)}) copy-start(f32[8,256]{1,0:T(8,128)} %copy-done.5) | copy-start | bytes 24580
  592.5 7.6 %copy-start.8 = (f32[8,256]{1,0:T(8,128)S(1)}, f32[8,256]{1,0:T(8,128)}, u32[]{:S(2)}) copy-start(f32[8,256]{1,0:T(8,128)} %copy-done.7) | copy-start | bytes 24580
  592.5 7.6 %copy-start.10 = (f32[8,256]{1,0:T(8,128)S(1)}, f32[8,256]{1,0:T(8,128)}, u32[]{:S(2)}) copy-start(f32[8,256]{1,0:T(8,128)} %copy-done.9) | copy-start | bytes 24580
  592.5 7.6 %copy-start.12 = (f32[8,256]{1,0:T(8,128)S(1)}, f32[8,256]{1,0:T(8,128)}, u32[]{:S(2)}) copy-start(f32[8,256]{1,0:T(8,128)} %copy-done.11) | copy-start | bytes 24580
  592.5 7.6 %copy-start.20 = (pred[256]{0:T(512)(128)(4,1)S(1)}, pred[256]{0:T(512)(128)(4,1)}, u32[]{:S(2)}) copy-start(pred[256]{0:T(512)(128)(4,1)} %get-tuple-element.2189) | copy-start | bytes 772
  592.5 7.6 %copy-start.22 = (pred[256]{0:T(512)(128)(4,1)S(1)}, pred[256]{0:T(512)(128)(4,1)}, u32[]{:S(2)}) copy-start(pred[256]{0:T(512)(128)(4,1)} %get-tuple-element.2190) | copy-start | bytes 772
  595.8 5.6 copy-start.14
Sparse Core Ops, SparseCore 0:
  11.9 136.8 all-gather.18
  253.2 37.5 all-gather.14
  292.9 32.5 all-gather.16
  327.5 32.5 all-gather.12
  451.7 131.2 all-gather.20
where the time goes:
time: 710 us; the launch traced here: 704 us
  waiting for transfers between devices  277 us (39%)
  other arithmetic  217 us (31%)
  local copies, waits for them, and re-layouts  113 us (16%)
  blocking collectives  71.2 us (10%)
  between operations  14.1 us (2%)
  loops' own time  11.5 us (2%)
    all_gather x2, waiting for transfers between devices, ghost_term(): all_faces = lax.all_gather(own_faces, 'surf', axis=0, tiled=True)  216 us
    reduce_sum x87, other arithmetic, product(): return jnp.sum(left_mat[:, :, None, :] * right_mat[None, :, :, :], axis=1)  59.1 us
    all_gather x2, blocking collectives, sweep(): lax.all_gather(tip_term[None], 'line', axis=0, tiled=True)  45.7 us
    reduce_sum x35, other arithmetic, product_vec(): return jnp.sum(matrix * vector[None, :, :], axis=1)  33.2 us
    all_gather x1, waiting for transfers between devices, segment_lines(): lax.all_gather(own_block[None], 'line', axis=0, tiled=True)  31.7 us
    mul x30, local copies, waits for them, and re-layouts, product(): return jnp.sum(left_mat[:, :, None, :] * right_mat[None, :, :, :], axis=1)  28.2 us
    all_gather x1, waiting for transfers between devices, segment_lines(): lax.all_gather(cross_block[None], 'line', axis=0, tiled=True)  27.9 us
    all_gather x2, blocking collectives, sweep(): lax.all_gather(own_source[None], 'line', axis=0, tiled=True)  25.5 us
  transfers between devices with their start and end apart: 5, of which 4 were waited for; matrix products, arithmetic and copies ran while one was open for 8% of the time, Pallas kernels for 0%

commit v1 on v0

v1 whole, which is shorter than its diff:
```python
import functools

import jax
import jax.numpy as jnp
from jax import lax
from jax.experimental import pallas as pl
from jax.experimental.pallas import tpu as pltpu
from jax.sharding import PartitionSpec as P

N = 13
PW = 16
NY = 4
NZ = 16
NLINE = 8
FB = 56
MROWS = 176
VROWS = 16
MESH = pl.DeviceIdType.MESH
F32 = jnp.float32
BF16 = jnp.bfloat16


def sub_of(shape):
    return lax.broadcasted_iota(jnp.int32, shape, len(shape) - 2)


def lane_of(shape):
    return lax.broadcasted_iota(jnp.int32, shape, len(shape) - 1)


def sroll(x, k):
    return pltpu.roll(x, k % 8, x.ndim - 2)


def lroll(x, k):
    return pltpu.roll(x, k % x.shape[-1], x.ndim - 1)


def mm(out, a, b, ta=False):
    def rows(at):
        acc = [None] * len(at)
        for k in range(N):
            bk = b[k]
            for n, i in enumerate(at):
                term = (a[k, i] if ta else a[i, k])[None] * bk
                acc[n] = term if k == 0 else acc[n] + term
        for n, i in enumerate(at):
            out[i] = acc[n]

    def pair(q, carry):
        rows([2 * q, 2 * q + 1])
        return carry

    lax.fori_loop(0, N // 2, pair, 0)
    rows([N - 1])


def inverse(src, dst):
    a = [src[i, pl.ds(i, N - i)] for i in range(N)]
    for p in range(N):
        d = 1.0 / a[p][0:1]
        parts = [a[i][p - i : p - i + 1] for i in range(p)] + [a[p]]
        col = jnp.concatenate(parts, axis=0) if p else a[p]
        scaled = col * d
        for i in range(N):
            if i == p:
                continue
            new = a[i] - col[i : i + 1] * scaled[i:]
            if i < p:
                pieces = [new[: p - i], scaled[i : i + 1]]
                if p - i + 1 < N - i:
                    pieces.append(new[p - i + 1 :])
                new = jnp.concatenate(pieces, axis=0)
            a[i] = new
        a[p] = jnp.concatenate([-d, scaled[p + 1 :]], axis=0) if p + 1 < N else -d
    for i in range(N):
        neg = -a[i]
        dst[i, pl.ds(i, N - i)] = neg
        for j in range(i + 1, N):
            dst[j, i] = neg[j - i]


def mvt(g, x):
    acc = x[0:1] * g[0]
    for k in range(1, N):
        acc = acc + x[k : k + 1] * g[k]
    return acc


def mv(g, x):
    acc = x[0:1] * g[:, 0]
    for k in range(1, N):
        acc = acc + x[k : k + 1] * g[:, k]
    return acc


def exchange_groups(v):
    which = (lane_of((8, 128)) // 32 - sub_of((8, 128)) // 2 + 4) % 4
    out = v
    for step in range(1, 4):
        out = jnp.where((which == step)[None], sroll(lroll(v, 32 * step), -2 * step), out)
    return out


def split_cells(v):
    h0, h1 = v[:, :, :128], v[:, :, 128:]
    even = (sub_of((8, 128)) % 2 == 0)[None]
    return jnp.where(even, h0, sroll(h1, 1)), jnp.where(even, sroll(h0, -1), h1)


def join_cells(xe, xo):
    even = (sub_of((8, 128)) % 2 == 0)[None]
    h0 = jnp.where(even, xe, sroll(xo, 1))
    h1 = jnp.where(even, sroll(xe, -1), xo)
    return jnp.concatenate([h0, h1], axis=2)


def three_parts(x):
    high = x.astype(BF16).astype(F32)
    rest = x - high
    mid = rest.astype(BF16).astype(F32)
    return jnp.concatenate([high, mid, rest - mid], axis=0).astype(BF16)


def kernel(
    res, prev, edge, damp, lat, coup, flags, gain, tab_v, tab_s, out,
    mats, work, zg0, zg1, yb0, yb1, ysend, tscr, tsm, pick, spread, lsc, wts, inner, field,
    fs, fr, vs, vr, bs, br,
    zss, zrs, yss, yrs, tss, trs, fss, frs, vss, vrs, bss, brs, lsem,
):
    zgs, ybs = (zg0, zg1), (yb0, yb1)
    place = lax.axis_index("line")
    patch = lax.axis_index("surf")
    z, y = patch // NY, patch % NY

    def line_dev(k):
        return (lax.rem(place + k, NLINE), patch)

    def z_dev(k):
        return (place, lax.rem(z + k + NZ, NZ) * NY + y)

    def y_dev(k):
        return (place, z * NY + lax.rem(y + k, NY))

    barrier = pltpu.get_barrier_semaphore()
    friends = [line_dev(k) for k in range(1, NLINE)]
    friends += [z_dev(k) for k in (1, 2, 3, -1, -2, -3)]
    friends += [y_dev(k) for k in range(1, NY)]
    for friend in friends:
        pl.semaphore_signal(barrier, inc=1, device_id=friend, device_id_type=MESH)

    sent = []

    def send(src, dst, ssem, rsem, target):
        copy = pltpu.make_async_remote_copy(
            src_ref=src, dst_ref=dst, send_sem=ssem, recv_sem=rsem, device_id=target, device_id_type=MESH
        )
        copy.start()
        sent.append(copy)
        return copy

    tile = (8, 128)
    sub, lane = sub_of(tile), lane_of(tile)
    slot = sub // 2

    line = lax.broadcasted_iota(jnp.int32, (512, 128), 0)
    col = lax.broadcasted_iota(jnp.int32, (512, 128), 1)
    face, pos = (col // 16) % 4, col % 16
    row_at, col_at = (line % 256) // PW, line % PW
    across = jnp.where(face < 2, row_at, col_at)
    along = jnp.where(face < 2, col_at, row_at)
    hit = (across == (face % 2) * (PW - 1)) & (along == pos) & (line // 256 == col // 64)
    pick[...] = jnp.where(hit, 1.0, 0.0).astype(BF16)

    def borders(values):
        low = values[0:7].reshape(FB, 256)
        high = jnp.concatenate([values[7:N], jnp.zeros((1, 8, 256), F32)], axis=0).reshape(FB, 256)
        wide = jnp.concatenate([low, high], axis=1)
        got = jnp.dot(three_parts(wide), pick[...], preferred_element_type=F32)
        return got[0:FB] + got[FB : 2 * FB] + got[2 * FB :]

    def z_send(ph, d, dist, hop):
        at = lax.rem(z - d * (dist - hop) + NZ, NZ)
        side = 0 if d > 0 else 1
        return send(
            zgs[ph].at[at], zgs[ph].at[at], zss.at[ph, side, dist - 1], zrs.at[ph, side, dist - 1], z_dev(d * hop)
        )

    def z_step(ph, number, flying):
        if number == 0:
            plan = [(d, hop, hop) for hop in (3, 2, 1) for d in (1, -1)]
        elif number == 1:
            for d in (1, -1):
                flying.pop((d, 3)).wait_recv()
            plan = [(d, 3 + hop, hop) for hop in (3, 2, 1) for d in (1, -1)]
        else:
            for d in (1, -1):
                flying.pop((d, 6)).wait_recv()
            plan = [(1, 8, 2), (1, 7, 1), (-1, 7, 1)]
        for d, dist, hop in plan:
            flying[(d, dist)] = z_send(ph, d, dist, hop)

    group = (lane_of((FB, 128)) // 16) % 4

    def choose(blocks):
        got = jnp.where(group == 1, blocks[0], jnp.where(group == 0, blocks[1], jnp.where(group == 3, blocks[2], blocks[3])))
        return got

    def y_phase(ph, flying):
        for copy in flying.values():
            copy.wait_recv()
        arriving = []
        for k in (2, 1, 3, 0):
            to = lax.rem(y + k, NY)
            block = choose([zgs[ph][tsm[to, 0, f] // NY] for f in range(4)])
            if k == 0:
                ybs[ph][y] = block
            else:
                ysend[ph, k - 1] = block
                arriving.append(
                    send(ysend.at[ph, k - 1], ybs[ph].at[y], yss.at[ph, k - 1], yrs.at[ph, k - 1], y_dev(k))
                )
        return arriving

    def ghosts(ph, arriving):
        for copy in arriving:
            copy.wait_recv()
        block = choose([ybs[ph][tsm[y, 0, f] % NY] for f in range(4)])
        got = jnp.dot(three_parts(block), spread[...], preferred_element_type=F32)
        got = got[0:FB] + got[FB : 2 * FB] + got[2 * FB :]
        return got

    def all_to_all(src, dst, rows, ssem, rsem):
        own = pl.multiple_of(place * rows, 8)
        arriving = []
        for k in (4, 3, 5, 2, 6, 1, 7):
            to = pl.multiple_of(lax.rem(place + k, NLINE) * rows, 8)
            arriving.append(
                send(src.at[pl.ds(to, rows)], dst.at[pl.ds(own, rows)], ssem.at[k - 1], rsem.at[k - 1], line_dev(k))
            )
        dst[pl.ds(own, rows)] = src[pl.ds(own, rows)]
        return arriving

    zg0[z] = borders(prev[...])
    tscr[y] = jnp.zeros(tile, jnp.int32)
    tscr[y, 0:2, 0:4] = tab_v[...]
    pl.semaphore_wait(barrier, len(friends))
    flying = {}
    z_step(0, 0, flying)
    tables = [send(tscr.at[y], tscr.at[y], tss.at[k - 1], trs.at[k - 1], y_dev(k)) for k in range(1, NY)]

    (uo, ue, pm, dd, v1, gl, gr, c1, sl, sr, x2, v2, g2, s2, c2, x3, v3, g3, s3, c3, rc, rd,
     w1, h1, x1r, w2, h2, w3, h3, w4) = [mats.at[n] for n in range(30)]

    def each_row(body):
        def step(i, carry):
            body(i)
            return carry

        lax.fori_loop(0, N, step, 0)

    first = ((sub < 2) & (place == 0))[None]
    even_sub = (sub % 2 == 0)[None]

    def build(i):
        e = edge[i].astype(F32)
        h0, h1 = e[:, :, :128], e[:, :, 128:]
        u = jnp.where(even_sub, h0, sroll(h1, 1))
        o = jnp.where(even_sub, sroll(h0, -1), h1)
        uo[i] = o
        ue[i] = jnp.where(first, 0.0, u)
        pm[i] = u + o
        dd[i] = o + jnp.where((sub < 6)[None], sroll(u, -2), 0.0)

    each_row(build)
    de, do = split_cells(damp[...])
    flag = flags[...].astype(F32)
    wall = jnp.where(sub == 0, flag[:, :128], flag[:, 128:])
    wall = jnp.where(first[0], wall, 0.0)
    for i in range(N):
        pm[i, i] = pm[i, i] + de[i] + wall * gain[i]
        dd[i, i] = dd[i, i] + do[i]
    inverse(pm, v1)
    z_step(0, 1, flying)
    mm(gl, v1, ue)
    mm(gr, v1, uo)
    mm(sl, ue, gl)
    mm(sr, uo, gr)
    mm(c1, ue, gr)
    z_step(0, 2, flying)

    def level(p, x, v, g, s, c, shift):
        inverse(p, v)
        mm(g, v, x)
        mm(s, x, g, True)
        if c is not None:

            def turn(i):
                work[i] = sroll(g[i], -shift)

            each_row(turn)
            mm(c, x, work, True)

    def build(i):
        d = dd[i] - sr[i] - jnp.where((sub < 6)[None], sroll(sl[i], -2), 0.0)
        dd[i] = d
        even = (slot % 2 == 0)[None]
        pm[i] = jnp.where(even, d, sroll(d, 2))
        x2[i] = jnp.where(even, c1[:, i], c1[i])

    each_row(build)
    level(pm, x2, v2, g2, s2, c2, 2)

    for copy in tables:
        copy.wait_recv()
    to_smem = pltpu.make_async_copy(tscr, tsm, lsem)
    to_smem.start()
    to_smem.wait()
    arriving = y_phase(0, flying)

    def build(i):
        d = dd[i] - s2[i] - jnp.where((slot == 1)[None], sroll(s2[i], -2), 0.0)
        dd[i] = d
        low = (slot == 0)[None]
        pm[i] = jnp.where(low, sroll(d, -2), sroll(d, 2))
        x3[i] = jnp.where(low, c2[:, i], c2[i])

    each_row(build)
    level(pm, x3, v3, g3, s3, c3, 4)

    def build(i):
        own = dd[i] - sroll(s3[i], 2)
        push = ue[i] - sl[i] - s2[i] - s3[i]
        v = jnp.where((slot == 0)[None], c3[i], jnp.where((slot == 1)[None], sroll(push, 2), own))
        v = exchange_groups(jnp.where((slot == 2)[None], 0.0, v))
        for j in range(N):
            fs[pl.ds(i * N + j, 8, stride=MROWS), :] = v[j]

    each_row(build)
    blocks = all_to_all(fs, fr, MROWS, fss, frs)

    src = lax.broadcasted_iota(jnp.int32, (128, 1024), 0)
    dst = lax.broadcasted_iota(jnp.int32, (128, 1024), 1)
    face = ((src // 16) % 4) ^ 1
    turned = jnp.where(face == 0, tab_s[1, 0], jnp.where(face == 1, tab_s[1, 1], jnp.where(face == 2, tab_s[1, 2], tab_s[1, 3])))
    line = dst % 256
    across = jnp.where(face < 2, line // PW, line % PW)
    along = jnp.where(face < 2, line % PW, line // PW)
    along = along + turned * (PW - 1 - 2 * along)
    hit = (across == (face % 2) * (PW - 1)) & (along == src % 16)
    hit = hit & (dst // 512 == src // 64) & ((dst // 256) % 2 == face // 2)
    spread[...] = jnp.where(hit, 1.0, 0.0).astype(BF16)

    for c in range(8):
        for h in range(2):
            lsc[h, pl.ds(4 * c, 4), :] = lat[c, :, pl.ds(128 * h, 128)]
    lats = [
        jnp.concatenate([lsc[h, pl.ds(d, 8, stride=4), :] for h in range(2)], axis=1) for d in range(4)
    ]
    line = lane_of((8, 256))
    edges = [line < PW, line >= 256 - PW, line % PW == 0, line % PW == PW - 1]
    for d in range(4):
        wts[d] = jnp.where(edges[d], 0.0, lats[d])
    for kind in range(2):
        wts[4 + kind] = jnp.where(
            edges[2 * kind], lats[2 * kind], jnp.where(edges[2 * kind + 1], lats[2 * kind + 1], 0.0)
        )

    def inside(v):
        for i in range(N):
            x = v[i]
            inner[i] = (
                wts[0] * lroll(x, PW) + wts[1] * lroll(x, -PW) + wts[2] * lroll(x, 1) + wts[3] * lroll(x, -1)
            )

    def right_side(got):
        weighted = []
        for i in range(N):
            at, base = (8 * i, 0) if i < 7 else (8 * (i - 7), 512)
            weighted.append(
                inner[i] + wts[4] * got[at : at + 8, base : base + 256] + wts[5] * got[at : at + 8, base + 256 : base + 512]
            )
        rows = []
        for a in range(N):
            acc = res[a]
            for b in range(N):
                acc = acc - coup[a, b] * weighted[b]
            rows.append(acc[None])
        return jnp.concatenate(rows, axis=0)

    def forward(ph, rhs):
        re, ro = split_cells(rhs)
        ul, ur = mvt(gl, re), mvt(gr, re)
        ro = ro + ur + jnp.where((sub < 6)[None], sroll(ul, -2), 0.0)
        rk2 = jnp.where((slot % 2 == 0)[None], ro, sroll(ro, 2))
        u2 = mvt(g2, rk2)
        ro = ro + u2 + jnp.where((slot == 1)[None], sroll(u2, -2), 0.0)
        rk3 = jnp.where((slot == 0)[None], sroll(ro, -2), sroll(ro, 2))
        u3 = mvt(g3, rk3)
        own = ro + sroll(u3, 2)
        tip = ul + u2 + u3
        v = jnp.where((slot == 1)[None], sroll(tip, 2), jnp.where((slot == 3)[None], own, 0.0))
        v = exchange_groups(v)
        for j in range(N):
            vs[ph, pl.ds(j, 8, stride=VROWS), :] = v[j]
        for j in range(N, VROWS):
            vs[ph, pl.ds(j, 8, stride=VROWS), :] = jnp.zeros(tile, F32)
        arriving = all_to_all(vs.at[ph], vr.at[ph], VROWS, vss.at[ph], vrs.at[ph])
        return re, rk2, rk3, arriving

    def separators(ph, arriving):
        for copy in arriving:
            copy.wait_recv()
        got = jnp.concatenate([vr[ph, pl.ds(j, 8, stride=VROWS), :][None] for j in range(N)], axis=0)
        r = lroll(got, 32) + jnp.where((sub < 7)[None], sroll(lroll(got, 96), -1), 0.0)
        even = (sub % 2 == 0)[None]
        fourth = (sub % 4 == 0)[None]
        rk1 = jnp.where(even, r, sroll(r, 1))
        u = mvt(h1, rk1)
        r = r + u + sroll(u, -1)
        rk2 = jnp.where(fourth, sroll(r, -1), sroll(r, 1))
        u = mvt(h2, rk2)
        r = r + sroll(u, 1) + sroll(u, -1)
        rk3 = sroll(r, 1)
        u = mvt(h3, rk3)
        x7 = mvt(w4, r + sroll(u, 3))
        x3 = sroll(mvt(w3, rk3) + mv(h3, sroll(x7, -3)), -1)
        known = jnp.where((sub == 3)[None], x3, x7)
        near = jnp.where((sub == 2)[None], sroll(x3, -1), jnp.where((sub == 4)[None], sroll(x3, 1), sroll(x7, -1)))
        near = jnp.where((sub == 0)[None], 0.0, near)
        u = mv(h2, near) + jnp.where(fourth, mvt(w2, rk2), 0.0)
        x = jnp.where((sub % 4 == 1)[None], sroll(u, 1) + sroll(u, -1), known)
        near = jnp.where((sub == 0)[None], 0.0, jnp.where(even, sroll(x, 1), x))
        u = mv(h1, near) + jnp.where(even, mvt(w1, rk1), 0.0)
        x = jnp.where(even, u + sroll(u, -1), x)
        below = jnp.where((sub == 0)[None], 0.0, sroll(x, 1))
        quarter = (lane // 32)[None]
        msg = jnp.where(
            quarter == 0, below, jnp.where(quarter == 2, lroll(x, 64), jnp.where(quarter == 3, lroll(x, 96), 0.0))
        )
        for j in range(N):
            bs[ph, pl.ds(j, 8, stride=VROWS), :] = msg[j]
        for j in range(N, VROWS):
            bs[ph, pl.ds(j, 8, stride=VROWS), :] = jnp.zeros(tile, F32)
        return all_to_all(bs.at[ph], br.at[ph], VROWS, bss.at[ph], brs.at[ph])

    def backward(ph, kept, arriving):
        re, rk2, rk3, _ = kept
        y1, y2, y3 = mvt(v1, re), mvt(v2, rk2), mvt(v3, rk3)
        for copy in arriving:
            copy.wait_recv()
        got = jnp.concatenate([br[ph, pl.ds(j, 8, stride=VROWS), :][None] for j in range(N)], axis=0)
        ends = exchange_groups(got)
        u = mv(g3, ends) + jnp.where((slot == 0)[None], y3, 0.0)
        x3 = sroll(u, 2) + sroll(u, -2)
        near = jnp.where((slot == 1)[None], x3, jnp.where((slot == 2)[None], sroll(x3, 2), ends))
        u = mv(g2, near) + jnp.where((slot % 2 == 0)[None], y2, 0.0)
        both = u + sroll(u, -2)
        xo = jnp.where((slot % 2 == 0)[None], both, jnp.where((slot == 1)[None], x3, ends))
        xl = jnp.where((slot == 0)[None], ends, sroll(xo, 2))
        xe = y1 + mv(gl, xl) + mv(gr, xo)
        return join_cells(xe, xo)

    inside(prev)
    rhs = right_side(ghosts(0, arriving))
    kept = forward(0, rhs)

    for copy in blocks:
        copy.wait_recv()

    def build(i):
        rows = []
        for j in range(N):
            rows.append(fr[pl.ds(i * N + j, 8, stride=MROWS), :][None])
        v = jnp.concatenate(rows, axis=0)
        rc[i] = v
        rd[i] = lroll(v, 32) + jnp.where((sub < 7)[None], sroll(lroll(v, 96), -1), 0.0)

    each_row(build)

    def build(i):
        even = (sub % 2 == 0)[None]
        x1r[i] = jnp.where(even, rc[:, i], rc[i])
        pm[i] = jnp.where(even, rd[i], sroll(rd[i], 1))

    each_row(build)
    level(pm, x1r, w1, h1, s3, c3, 1)

    def build(i):
        d = rd[i] - s3[i] - sroll(s3[i], -1)
        rd[i] = d
        fourth = (sub % 4 == 0)[None]
        pm[i] = jnp.where(fourth, sroll(d, -1), sroll(d, 1))
        x2[i] = jnp.where(fourth, c3[:, i], c3[i])

    each_row(build)
    level(pm, x2, w2, h2, s3, c2, 2)

    def build(i):
        d = rd[i] - sroll(s3[i], 1) - sroll(s3[i], -1)
        rd[i] = d
        pm[i] = sroll(d, 1)

    each_row(build)
    level(pm, c2, w3, h3, s3, None, 0)

    def build(i):
        pm[i] = rd[i] - sroll(s3[i], 3)

    each_row(build)
    inverse(pm, w4)

    back = separators(0, kept[3])
    first_sweep = backward(0, kept, back)
    zg1[z] = borders(first_sweep)
    field[...] = first_sweep
    flying = {}
    z_step(1, 0, flying)
    inside(field)
    z_step(1, 1, flying)
    z_step(1, 2, flying)
    arriving = y_phase(1, flying)
    rhs = right_side(ghosts(1, arriving))
    kept = forward(1, rhs)
    back = separators(1, kept[3])
    out[...] = backward(1, kept, back)

    for copy in sent:
        copy.wait_send()


def body(residual, previous, edge_blocks, damping, lateral, coupling, wall_flags, wall_gain, face_table):
    def by_unknown(v):
        return jnp.transpose(v, (1, 0, 2))

    table = jnp.transpose(face_table[0])
    vmem = pl.BlockSpec(memory_space=pltpu.VMEM)
    smem = pl.BlockSpec(memory_space=pltpu.SMEM)
    dma = pltpu.SemaphoreType.DMA
    got = pl.pallas_call(
        kernel,
        out_shape=jax.ShapeDtypeStruct((N, 8, 256), F32),
        in_specs=[vmem, vmem, vmem, vmem, vmem, smem, vmem, smem, vmem, smem],
        out_specs=vmem,
        scratch_shapes=[
            pltpu.VMEM((30, N, N, 8, 128), F32),
            pltpu.VMEM((N, N, 8, 128), F32),
            pltpu.VMEM((NZ, FB, 128), F32),
            pltpu.VMEM((NZ, FB, 128), F32),
            pltpu.VMEM((NY, FB, 128), F32),
            pltpu.VMEM((NY, FB, 128), F32),
            pltpu.VMEM((2, NY - 1, FB, 128), F32),
            pltpu.VMEM((NY, 8, 128), jnp.int32),
            pltpu.SMEM((NY, 8, 128), jnp.int32),
            pltpu.VMEM((512, 128), BF16),
            pltpu.VMEM((128, 1024), BF16),
            pltpu.VMEM((2, 32, 128), F32),
            pltpu.VMEM((6, 8, 256), F32),
            pltpu.VMEM((N, 8, 256), F32),
            pltpu.VMEM((N, 8, 256), F32),
            pltpu.VMEM((NLINE * MROWS, 128), F32),
            pltpu.VMEM((NLINE * MROWS, 128), F32),
            pltpu.VMEM((2, NLINE * VROWS, 128), F32),
            pltpu.VMEM((2, NLINE * VROWS, 128), F32),
            pltpu.VMEM((2, NLINE * VROWS, 128), F32),
            pltpu.VMEM((2, NLINE * VROWS, 128), F32),
            dma((2, 2, 8)),
            dma((2, 2, 8)),
            dma((2, NY - 1)),
            dma((2, NY - 1)),
            dma((NY - 1,)),
            dma((NY - 1,)),
            dma((NLINE - 1,)),
            dma((NLINE - 1,)),
            dma((2, NLINE - 1)),
            dma((2, NLINE - 1)),
            dma((2, NLINE - 1)),
            dma((2, NLINE - 1)),
            dma,
        ],
        compiler_params=pltpu.CompilerParams(
            collective_id=0, has_side_effects=True, vmem_limit_bytes=48 * 1024 * 1024
        ),
        name="line_sweeps",
    )(
        by_unknown(residual),
        by_unknown(previous),
        jnp.transpose(edge_blocks, (1, 2, 0, 3)),
        by_unknown(damping),
        lateral,
        coupling,
        wall_flags.reshape(1, 256),
        wall_gain,
        table,
        table,
    )
    return jnp.transpose(got, (1, 0, 2))


def solution(mesh):
    placed = (
        P("line", None, "surf"),
        P("line", None, "surf"),
        P("line", None, None, "surf"),
        P("line", None, "surf"),
        P("line", None, "surf"),
        P(),
        P("surf"),
        P(),
        P("surf", None, None),
    )
    return jax.shard_map(
        body, mesh=mesh, in_specs=placed, out_specs=P("line", None, "surf"), check_vma=False
    )
```

time: 710 us -> 90.4 us (0.13)
  waiting for transfers between devices: 277 us -> 0 us
  other arithmetic: 217 us -> 0 us
  local copies, waits for them, and re-layouts: 113 us -> 5.89 us
  Pallas kernels: 0 us -> 84.2 us
  blocking collectives: 71.2 us -> 0 us
  between operations: 14.1 us -> 0.03 us
  loops' own time: 11.5 us -> 0 us
    all_gather x5 -> x0, waiting for transfers between devices: 276 us -> none  [the longest x2 216 us: ghost_term(): all_faces = lax.all_gather(own_faces, 'surf', axis=0, tiled=True)]
    reduce_sum x150 -> x0, other arithmetic: 112 us -> none  [the longest x87 59.1 us: product(): return jnp.sum(left_mat[:, :, None, :] * right_mat[None, :, :, :], axis=1)]
    pallas_call x0 -> x1, Pallas kernels: none -> 84.2 us  [body(): pl.pallas_call(kernel, out_shape=jax.ShapeDtypeStruct((N, 8, 256), F32),...]
    all_gather x4 -> x0, blocking collectives: 71.2 us -> none  [the longest x2 45.7 us: sweep(): lax.all_gather(tip_term[None], 'line', axis=0, tiled=True)]
    mul x42 -> x0, local copies, waits for them, and re-layouts: 35.9 us -> none  [the longest x30 28.2 us: product(): return jnp.sum(left_mat[:, :, None, :] * right_mat[None, :, :, :], axis=1)]
    sub x246 -> x0, other arithmetic: 33.6 us -> none  [the longest x180 9.3 us: invert(): matrix - column[:, None] * row_mat[None]]
    add x31 -> x0, other arithmetic: 26 us -> none  [the longest x21 18.3 us: interior_backward(): solved = partial_value + product(gain_here, carried)]
    dynamic_update_slice x52 -> x0, local copies, waits for them, and re-layouts: 22.4 us -> none  [the longest x21 10.1 us: interior_solve(): lax.scan(forward, jnp.zeros_like(sources[0]), (inverses, lowers, sources))]
  transfers between devices with their start and end apart: 5 -> 0, of which waited for: 4 -> 0; matrix products, arithmetic and copies ran while one was open for 8% -> 0% of each run, Pallas kernels for 0% -> 0%
where the time goes in v1:
time: 90.4 us; the launch traced here: 90.1 us
  Pallas kernels  84.2 us (93%)
  local copies, waits for them, and re-layouts  5.89 us (7%)
    pallas_call x1, Pallas kernels, body(): pl.pallas_call(kernel, out_shape=jax.ShapeDtypeStruct((N, 8, 256), F32),...  84.2 us
    unnamed x19, local copies, waits for them, and re-layouts  5.89 us

profile of v1, /device:TPU:1, one launch (start us, length us, event | category | flops | bytes accessed | tf_op | source)
XLA Modules:
  0.0 90.1 jit_solution(7807678777460507694)
XLA Ops:
  0.0 0.0 copy-start.5
  0.0 0.0 copy-start.7
  0.0 0.0 copy-start.6
  0.0 0.0 copy-start.8
  0.0 0.7 copy-done.5
  0.7 0.0 copy-done.7
  0.7 0.0 copy-done.6
  0.7 0.0 copy-done.8
  0.7 0.0 copy-start
  0.7 1.1 %copy-done = bf16[8,13,13,256]{3,0,2,1:T(8,128)(2,1)S(1)} copy-done((bf16[8,13,13,256]{3,0,2,1:T(8,128)(2,1)S(1)}, bf16[8,13,13,256]{3,0,2,1:T(8,128)(2,1)}, u32[]{:S(2)}) %copy-start) | copy-done | bytes 692248
  1.8 0.0 copy-start.1
  1.8 0.9 copy-done.1
  2.7 0.0 copy-start.2
  2.7 0.9 copy-done.2
  3.6 0.0 copy-start.3
  3.6 0.9 copy-done.3
  4.5 0.0 copy-start.4
  4.5 0.8 copy-done.4
  5.3 84.2 %line_sweeps.1 = f32[13,8,256]{2,1,0:T(8,128)S(1)} custom-call(f32[13,8,256]{2,1,0:T(8,128)S(1)} %bitcast.11, f32[13,8,256]{2,1,0:T(8,128)S(1)} %bitcast.12, bf16[13,13,8,256]{3,2,1,0:T(8,128)(2,1)S(1)} %bitcast.9, f32[13,8,256]{2,1,0:T(8,128)S(1)} %bitcast.13, f32[8,4,256]{2,1,0:T(4,128)S(1)} %copy-done.4, f32[13,13]{1,0:T(8,128)S(1)} %copy-done.5, ...), custom_call_target="tpu_custom_call" | custom-call | tf_op jit(solution)/shard_map/line_sweeps/pallas_call | solution.py:540
  89.5 0.6 copy.11
Async XLA Ops:
  0.0 0.7 copy-start.5
  0.0 0.7 copy-start.7
  0.0 0.7 copy-start.6
  0.0 0.7 copy-start.8
  0.7 1.1 %copy-start = (bf16[8,13,13,256]{3,0,2,1:T(8,128)(2,1)S(1)}, bf16[8,13,13,256]{3,0,2,1:T(8,128)(2,1)}, u32[]{:S(2)}) copy-start(bf16[8,13,13,256]{3,0,2,1:T(8,128)(2,1)} %param.11) | copy-start | bytes 2076676
  1.8 0.9 copy-start.1
  2.7 0.9 copy-start.2
  3.6 0.9 copy-start.3
  4.5 0.8 copy-start.4

commit v2 on v1

--- a/solution.py
+++ b/solution.py
@@ -13,7 +13,7 @@
 NZ = 16
 NLINE = 8
 FB = 56
-MROWS = 176
+MROWS = 96
 VROWS = 16
 MESH = pl.DeviceIdType.MESH
 F32 = jnp.float32
@@ -53,6 +53,46 @@
 
     lax.fori_loop(0, N // 2, pair, 0)
     rows([N - 1])
+
+
+def mm_upper(out, a, b):
+    for top in range(0, N, 2):
+        at = [i for i in (top, top + 1) if i < N]
+        acc = [None] * len(at)
+        for k in range(N):
+            bk = b[k, pl.ds(top, N - top)]
+            for n, i in enumerate(at):
+                term = a[k, i][None] * bk
+                acc[n] = term if k == 0 else acc[n] + term
+        for n, i in enumerate(at):
+            out[i, pl.ds(top, N - top)] = acc[n]
+
+
+def mm_split(out, a, b, ta=False, shift=0, upper=False):
+    for at in (range(0, 4), range(4, 8), range(8, N)):
+        low = at[0] // 4 if upper else 0
+        acc = [None] * len(at)
+        for k in range(N):
+            bk = b[k, pl.ds(low, 4 - low)]
+            if shift:
+                bk = sroll(bk, -shift)
+            for n, i in enumerate(at):
+                term = (a[k, i] if ta else a[i, k])[None] * bk
+                acc[n] = term if k == 0 else acc[n] + term
+        for n, i in enumerate(at):
+            out[i, pl.ds(low, 4 - low)] = acc[n]
+
+
+def spread_groups(v):
+    turns = [v] + [lroll(v, 32 * k) for k in range(1, 4)]
+    quarter = (lane_of((8, 128)) // 32)[None]
+    got = []
+    for g in range(4):
+        x = turns[3]
+        for k in range(3):
+            x = jnp.where(quarter == (g + k) % 4, turns[k], x)
+        got.append(x)
+    return got
 
 
 def inverse(src, dst):
@@ -123,12 +163,17 @@
 
 
 def kernel(
-    res, prev, edge, damp, lat, coup, flags, gain, tab_v, tab_s, out,
-    mats, work, zg0, zg1, yb0, yb1, ysend, tscr, tsm, pick, spread, lsc, wts, inner, field,
+    res_any, prev_any, edge_any, damp_any, lat_any, coup, flags, gain, tab_v, tab_s, out,
+    res, prev, edge, damp, lat, ins, mats, work, thin, zg0, zg1, yb0, yb1, ysend, tscr, tsm, pick, spread, lsc, wts, inner, field,
     fs, fr, vs, vr, bs, br,
     zss, zrs, yss, yrs, tss, trs, fss, frs, vss, vrs, bss, brs, lsem,
 ):
     zgs, ybs = (zg0, zg1), (yb0, yb1)
+    loads = {}
+    pairs = dict(prev=(prev_any, prev), edge=(edge_any, edge), damp=(damp_any, damp), lat=(lat_any, lat), res=(res_any, res))
+    for n, (name, (far, near)) in enumerate(pairs.items()):
+        loads[name] = pltpu.make_async_copy(far, near, ins.at[n])
+        loads[name].start()
     place = lax.axis_index("line")
     patch = lax.axis_index("surf")
     z, y = patch // NY, patch % NY
@@ -187,18 +232,20 @@
         )
 
     def z_step(ph, number, flying):
-        if number == 0:
-            plan = [(d, hop, hop) for hop in (3, 2, 1) for d in (1, -1)]
-        elif number == 1:
+        waited, plan = (
+            (0, ((3, 3), (1, 1))),
+            (1, ((2, 1),)),
+            (3, ((6, 3), (4, 1))),
+            (4, ((5, 1),)),
+            (6, ((8, 2), (7, 1))),
+        )[number]
+        if waited:
             for d in (1, -1):
-                flying.pop((d, 3)).wait_recv()
-            plan = [(d, 3 + hop, hop) for hop in (3, 2, 1) for d in (1, -1)]
-        else:
+                flying.pop((d, waited)).wait_recv()
+        for dist, hop in plan:
             for d in (1, -1):
-                flying.pop((d, 6)).wait_recv()
-            plan = [(1, 8, 2), (1, 7, 1), (-1, 7, 1)]
-        for d, dist, hop in plan:
-            flying[(d, dist)] = z_send(ph, d, dist, hop)
+                if d > 0 or dist < 8:
+                    flying[(d, dist)] = z_send(ph, d, dist, hop)
 
     group = (lane_of((FB, 128)) // 16) % 4
 
@@ -241,6 +288,7 @@
         dst[pl.ds(own, rows)] = src[pl.ds(own, rows)]
         return arriving
 
+    loads["prev"].wait()
     zg0[z] = borders(prev[...])
     tscr[y] = jnp.zeros(tile, jnp.int32)
     tscr[y, 0:2, 0:4] = tab_v[...]
@@ -257,7 +305,7 @@
             body(i)
             return carry
 
-        lax.fori_loop(0, N, step, 0)
+        lax.fori_loop(0, N, step, 0, unroll=True)
 
     first = ((sub < 2) & (place == 0))[None]
     even_sub = (sub % 2 == 0)[None]
@@ -272,7 +320,9 @@
         pm[i] = u + o
         dd[i] = o + jnp.where((sub < 6)[None], sroll(u, -2), 0.0)
 
-    each_row(build)
+    loads["edge"].wait()
+    each_row(build)
+    loads["damp"].wait()
     de, do = split_cells(damp[...])
     flag = flags[...].astype(F32)
     wall = jnp.where(sub == 0, flag[:, :128], flag[:, 128:])
@@ -281,25 +331,56 @@
         pm[i, i] = pm[i, i] + de[i] + wall * gain[i]
         dd[i, i] = dd[i, i] + do[i]
     inverse(pm, v1)
-    z_step(0, 1, flying)
     mm(gl, v1, ue)
     mm(gr, v1, uo)
-    mm(sl, ue, gl)
-    mm(sr, uo, gr)
+    z_step(0, 1, flying)
+    mm_upper(sl, ue, gl)
+    mm_upper(sr, uo, gr)
+    z_step(0, 2, flying)
     mm(c1, ue, gr)
-    z_step(0, 2, flying)
+    z_step(0, 3, flying)
 
     def level(p, x, v, g, s, c, shift):
         inverse(p, v)
         mm(g, v, x)
-        mm(s, x, g, True)
+        mm_upper(s, x, g)
+
+        def turn(i):
+            work[i] = sroll(g[i], -shift)
+
+        each_row(turn)
+        mm(c, x, work, True)
+
+    def level_split(p, x, v, g, s, c, shift):
+        inverse(p, v)
+        xs, gs, ss, cs = [thin.at[n] for n in range(4)]
+        quarter = lane // 32
+
+        def split(k):
+            for q in range(4):
+                got = x[k, 4 * q]
+                for n in range(1, min(4, N - 4 * q)):
+                    got = jnp.where(quarter == n, x[k, 4 * q + n], got)
+                xs[k, q] = got
+
+        each_row(split)
+        mm_split(gs, v, xs)
+        mm_split(ss, x, gs, True, upper=True)
         if c is not None:
-
-            def turn(i):
-                work[i] = sroll(g[i], -shift)
-
-            each_row(turn)
-            mm(c, x, work, True)
+            mm_split(cs, x, gs, True, shift)
+
+        def join(i):
+            for q in range(4):
+                wide = min(4, N - 4 * q)
+                full = spread_groups(ss[i, q][None])
+                far = spread_groups(cs[i, q][None]) if c is not None else None
+                for n in range(wide):
+                    g[i, 4 * q + n] = lroll(gs[i, q], -32 * n) if n else gs[i, q]
+                    s[i, 4 * q + n] = full[n][0]
+                    if c is not None:
+                        c[i, 4 * q + n] = far[n][0]
+
+        each_row(join)
 
     def build(i):
         d = dd[i] - sr[i] - jnp.where((sub < 6)[None], sroll(sl[i], -2), 0.0)
@@ -311,12 +392,11 @@
     each_row(build)
     level(pm, x2, v2, g2, s2, c2, 2)
 
+    z_step(0, 4, flying)
     for copy in tables:
         copy.wait_recv()
     to_smem = pltpu.make_async_copy(tscr, tsm, lsem)
     to_smem.start()
-    to_smem.wait()
-    arriving = y_phase(0, flying)
 
     def build(i):
         d = dd[i] - s2[i] - jnp.where((slot == 1)[None], sroll(s2[i], -2), 0.0)
@@ -330,14 +410,40 @@
 
     def build(i):
         own = dd[i] - sroll(s3[i], 2)
-        push = ue[i] - sl[i] - s2[i] - s3[i]
-        v = jnp.where((slot == 0)[None], c3[i], jnp.where((slot == 1)[None], sroll(push, 2), own))
-        v = exchange_groups(jnp.where((slot == 2)[None], 0.0, v))
-        for j in range(N):
-            fs[pl.ds(i * N + j, 8, stride=MROWS), :] = v[j]
-
-    each_row(build)
+        push = ue[:, i] - sl[:, i] - s2[:, i] - s3[:, i]
+        cross = c3[i]
+        rows = []
+        for q in range(7):
+            j = 2 * q
+            parts = [cross[j], jnp.where(j >= i, sroll(own[j], 4), sroll(push[j], 2))]
+            if j + 1 < N:
+                parts += [sroll(cross[j + 1], 4), jnp.where(j + 1 >= i, own[j + 1], sroll(push[j + 1], -2))]
+            else:
+                parts += [jnp.zeros(tile, F32)] * 2
+            v = parts[3]
+            for t in range(3):
+                v = jnp.where(slot == t, parts[t], v)
+            rows.append(v[None])
+        v = exchange_groups(jnp.concatenate(rows, axis=0))
+        for q in range(7):
+            fs[pl.ds(i * 7 + q, 8, stride=MROWS), :] = v[q]
+
+    each_row(build)
+    rows = []
+    for q in range(4):
+        v = jnp.zeros(tile, F32)
+        for t in range(min(4, N - 4 * q)):
+            i = 4 * q + t
+            v = jnp.where(slot == t, sroll(ue[i, i] - sl[i, i] - s2[i, i] - s3[i, i], 2 * t), v)
+        rows.append(v[None])
+    v = exchange_groups(jnp.concatenate(rows, axis=0))
+    for q in range(4):
+        fs[pl.ds(91 + q, 8, stride=MROWS), :] = v[q]
+    fs[pl.ds(95, 8, stride=MROWS), :] = jnp.zeros(tile, F32)
     blocks = all_to_all(fs, fr, MROWS, fss, frs)
+
+    to_smem.wait()
+    arriving = y_phase(0, flying)
 
     src = lax.broadcasted_iota(jnp.int32, (128, 1024), 0)
     dst = lax.broadcasted_iota(jnp.int32, (128, 1024), 1)
@@ -351,6 +457,8 @@
     hit = hit & (dst // 512 == src // 64) & ((dst // 256) % 2 == face // 2)
     spread[...] = jnp.where(hit, 1.0, 0.0).astype(BF16)
 
+    loads["lat"].wait()
+    loads["res"].wait()
     for c in range(8):
         for h in range(2):
             lsc[h, pl.ds(4 * c, 4), :] = lat[c, :, pl.ds(128 * h, 128)]
@@ -465,18 +573,27 @@
     rhs = right_side(ghosts(0, arriving))
     kept = forward(0, rhs)
 
+    rt = sr
     for copy in blocks:
         copy.wait_recv()
 
     def build(i):
-        rows = []
+        rows = [fr[pl.ds(i * 7 + q, 8, stride=MROWS), :][None] for q in range(7)]
+        got = spread_groups(jnp.concatenate(rows, axis=0))
         for j in range(N):
-            rows.append(fr[pl.ds(i * N + j, 8, stride=MROWS), :][None])
-        v = jnp.concatenate(rows, axis=0)
-        rc[i] = v
-        rd[i] = lroll(v, 32) + jnp.where((sub < 7)[None], sroll(lroll(v, 96), -1), 0.0)
-
-    each_row(build)
+            rc[i, j] = got[j % 2 * 2][j // 2]
+            rt[i, j] = got[j % 2 * 2 + 1][j // 2]
+
+    each_row(build)
+
+    def build(i):
+        rd[i] = rt[i] + jnp.where((sub < 7)[None], sroll(rt[:, i], -1), 0.0)
+
+    each_row(build)
+    rows = [fr[pl.ds(91 + q, 8, stride=MROWS), :][None] for q in range(4)]
+    got = spread_groups(jnp.concatenate(rows, axis=0))
+    for i in range(N):
+        rd[i, i] = rt[i, i] + jnp.where(sub < 7, sroll(got[i % 4][i // 4], -1), 0.0)
 
     def build(i):
         even = (sub % 2 == 0)[None]
@@ -484,7 +601,7 @@
         pm[i] = jnp.where(even, rd[i], sroll(rd[i], 1))
 
     each_row(build)
-    level(pm, x1r, w1, h1, s3, c3, 1)
+    level_split(pm, x1r, w1, h1, s3, c3, 1)
 
     def build(i):
         d = rd[i] - s3[i] - sroll(s3[i], -1)
@@ -494,7 +611,7 @@
         x2[i] = jnp.where(fourth, c3[:, i], c3[i])
 
     each_row(build)
-    level(pm, x2, w2, h2, s3, c2, 2)
+    level_split(pm, x2, w2, h2, s3, c2, 2)
 
     def build(i):
         d = rd[i] - sroll(s3[i], 1) - sroll(s3[i], -1)
@@ -502,7 +619,7 @@
         pm[i] = sroll(d, 1)
 
     each_row(build)
-    level(pm, c2, w3, h3, s3, None, 0)
+    level_split(pm, c2, w3, h3, s3, None, 0)
 
     def build(i):
         pm[i] = rd[i] - sroll(s3[i], 3)
@@ -517,8 +634,8 @@
     flying = {}
     z_step(1, 0, flying)
     inside(field)
-    z_step(1, 1, flying)
-    z_step(1, 2, flying)
+    for number in range(1, 5):
+        z_step(1, number, flying)
     arriving = y_phase(1, flying)
     rhs = right_side(ghosts(1, arriving))
     kept = forward(1, rhs)
@@ -536,15 +653,23 @@
     table = jnp.transpose(face_table[0])
     vmem = pl.BlockSpec(memory_space=pltpu.VMEM)
     smem = pl.BlockSpec(memory_space=pltpu.SMEM)
+    far = pl.BlockSpec(memory_space=pl.ANY)
     dma = pltpu.SemaphoreType.DMA
     got = pl.pallas_call(
         kernel,
         out_shape=jax.ShapeDtypeStruct((N, 8, 256), F32),
-        in_specs=[vmem, vmem, vmem, vmem, vmem, smem, vmem, smem, vmem, smem],
+        in_specs=[far, far, far, far, far, smem, vmem, smem, vmem, smem],
         out_specs=vmem,
         scratch_shapes=[
+            pltpu.VMEM((N, 8, 256), F32),
+            pltpu.VMEM((N, 8, 256), F32),
+            pltpu.VMEM((N, N, 8, 256), BF16),
+            pltpu.VMEM((N, 8, 256), F32),
+            pltpu.VMEM((8, 4, 256), F32),
+            dma((5,)),
             pltpu.VMEM((30, N, N, 8, 128), F32),
             pltpu.VMEM((N, N, 8, 128), F32),
+            pltpu.VMEM((4, N, 4, 8, 128), F32),
             pltpu.VMEM((NZ, FB, 128), F32),
             pltpu.VMEM((NZ, FB, 128), F32),
             pltpu.VMEM((NY, FB, 128), F32),
@@ -579,7 +704,7 @@
             dma,
         ],
         compiler_params=pltpu.CompilerParams(
-            collective_id=0, has_side_effects=True, vmem_limit_bytes=48 * 1024 * 1024
+            collective_id=0, has_side_effects=True, vmem_limit_bytes=58 * 1024 * 1024
         ),
         name="line_sweeps",
     )(

time: 90.4 us -> 75.8 us (0.84)
  Pallas kernels: 84.2 us -> 74 us
  local copies, waits for them, and re-layouts: 5.89 us -> 1.55 us
    pallas_call x1, Pallas kernels: 84.2 us -> 74 us  [body(): pl.pallas_call(kernel, out_shape=jax.ShapeDtypeStruct((N, 8, 256), F32),...]
    unnamed x19 -> x1, local copies, waits for them, and re-layouts: 5.89 us -> 1.55 us
where the time goes in v2:
time: 75.8 us; the launch traced here: 75.6 us
  Pallas kernels  74 us (98%)
  local copies, waits for them, and re-layouts  1.55 us (2%)
    pallas_call x1, Pallas kernels, body(): pl.pallas_call(kernel, out_shape=jax.ShapeDtypeStruct((N, 8, 256), F32),...  74 us
    unnamed x1, local copies, waits for them, and re-layouts  1.55 us

profile of v2, /device:TPU:1, one launch (start us, length us, event | category | flops | bytes accessed | tf_op | source)
XLA Modules:
  0.0 75.6 jit_solution(5091241891964077210)
XLA Ops:
  0.0 74.0 %line_sweeps.1 = f32[13,8,256]{2,1,0:T(8,128)} custom-call(f32[13,8,256]{2,1,0:T(8,128)} %bitcast.11, f32[13,8,256]{2,1,0:T(8,128)} %bitcast.12, bf16[13,13,8,256]{3,2,1,0:T(8,128)(2,1)} %bitcast.9, f32[13,8,256]{2,1,0:T(8,128)} %bitcast.13, f32[8,4,256]{2,1,0:T(4,128)} %lat_any.1, f32[13,13]{1,0:T(8,128)} %coup.1, s32[1,256]{1,0:T(1,128)} %bitcast.16, ...), custom_call_target="tpu_custom_call" | custom-call | tf_op jit(solution)/shard_map/line_sweeps/pallas_call | solution.py:658
  74.0 1.5 %copy.11 = f32[8,13,256]{2,0,1:T(8,128)} copy(f32[8,13,256]{2,0,1:T(8,128)} %bitcast.10) | data formatting | bytes 212992

commit v3 on v2

--- a/solution.py
+++ b/solution.py
@@ -14,7 +14,7 @@
 NLINE = 8
 FB = 56
 MROWS = 96
-VROWS = 16
+VROWS = 8
 MESH = pl.DeviceIdType.MESH
 F32 = jnp.float32
 BF16 = jnp.bfloat16
@@ -169,30 +169,31 @@
     zss, zrs, yss, yrs, tss, trs, fss, frs, vss, vrs, bss, brs, lsem,
 ):
     zgs, ybs = (zg0, zg1), (yb0, yb1)
+    place = lax.axis_index("line")
+    patch = lax.axis_index("surf")
+    z, y = patch // NY, patch % NY
+
+    def line_dev(k):
+        return (lax.rem(place + k, NLINE), patch)
+
+    def z_dev(k):
+        return (place, lax.rem(z + k + NZ, NZ) * NY + y)
+
+    def y_dev(k):
+        return (place, z * NY + lax.rem(y + k, NY))
+
+    barrier = pltpu.get_barrier_semaphore()
+    friends = [z_dev(k) for k in (4, -4, 3, -3, 2, -2, 1, -1)]
+    friends += [line_dev(k) for k in (4, 3, 5, 2, 6, 1, 7)]
+    friends += [y_dev(k) for k in (2, 1, 3)]
+    for friend in friends:
+        pl.semaphore_signal(barrier, inc=1, device_id=friend, device_id_type=MESH)
+
     loads = {}
     pairs = dict(prev=(prev_any, prev), edge=(edge_any, edge), damp=(damp_any, damp), lat=(lat_any, lat), res=(res_any, res))
     for n, (name, (far, near)) in enumerate(pairs.items()):
         loads[name] = pltpu.make_async_copy(far, near, ins.at[n])
         loads[name].start()
-    place = lax.axis_index("line")
-    patch = lax.axis_index("surf")
-    z, y = patch // NY, patch % NY
-
-    def line_dev(k):
-        return (lax.rem(place + k, NLINE), patch)
-
-    def z_dev(k):
-        return (place, lax.rem(z + k + NZ, NZ) * NY + y)
-
-    def y_dev(k):
-        return (place, z * NY + lax.rem(y + k, NY))
-
-    barrier = pltpu.get_barrier_semaphore()
-    friends = [line_dev(k) for k in range(1, NLINE)]
-    friends += [z_dev(k) for k in (1, 2, 3, -1, -2, -3)]
-    friends += [y_dev(k) for k in range(1, NY)]
-    for friend in friends:
-        pl.semaphore_signal(barrier, inc=1, device_id=friend, device_id_type=MESH)
 
     sent = []
 
@@ -203,6 +204,10 @@
         copy.start()
         sent.append(copy)
         return copy
+
+    def settle(count):
+        while len(sent) > count:
+            sent.pop(0).wait_send()
 
     tile = (8, 128)
     sub, lane = sub_of(tile), lane_of(tile)
@@ -225,27 +230,24 @@
         return got[0:FB] + got[FB : 2 * FB] + got[2 * FB :]
 
     def z_send(ph, d, dist, hop):
-        at = lax.rem(z - d * (dist - hop) + NZ, NZ)
-        side = 0 if d > 0 else 1
+        step = 1 - 2 * lax.rem(z, 2) if d == 0 else d
+        at = lax.rem(z - step * (dist - hop) + NZ, NZ)
         return send(
-            zgs[ph].at[at], zgs[ph].at[at], zss.at[ph, side, dist - 1], zrs.at[ph, side, dist - 1], z_dev(d * hop)
+            zgs[ph].at[at], zgs[ph].at[at], zss.at[ph, d + 1, dist - 1], zrs.at[ph, d + 1, dist - 1], z_dev(step * hop)
         )
 
     def z_step(ph, number, flying):
         waited, plan = (
-            (0, ((3, 3), (1, 1))),
-            (1, ((2, 1),)),
-            (3, ((6, 3), (4, 1))),
-            (4, ((5, 1),)),
-            (6, ((8, 2), (7, 1))),
+            (0, ((4, 4), (1, 1))),
+            (1, ((3, 2), (2, 1))),
+            (4, ((8, 4), (7, 3), (6, 2), (5, 1))),
         )[number]
         if waited:
             for d in (1, -1):
                 flying.pop((d, waited)).wait_recv()
         for dist, hop in plan:
-            for d in (1, -1):
-                if d > 0 or dist < 8:
-                    flying[(d, dist)] = z_send(ph, d, dist, hop)
+            for d in (0,) if dist == 8 else (1, -1):
+                flying[(d, dist)] = z_send(ph, d, dist, hop)
 
     group = (lane_of((FB, 128)) // 16) % 4
 
@@ -336,13 +338,12 @@
     z_step(0, 1, flying)
     mm_upper(sl, ue, gl)
     mm_upper(sr, uo, gr)
-    z_step(0, 2, flying)
     mm(c1, ue, gr)
-    z_step(0, 3, flying)
-
-    def level(p, x, v, g, s, c, shift):
+
+    def level(p, x, v, g, s, c, shift, between):
         inverse(p, v)
         mm(g, v, x)
+        between()
         mm_upper(s, x, g)
 
         def turn(i):
@@ -390,9 +391,7 @@
         x2[i] = jnp.where(even, c1[:, i], c1[i])
 
     each_row(build)
-    level(pm, x2, v2, g2, s2, c2, 2)
-
-    z_step(0, 4, flying)
+    level(pm, x2, v2, g2, s2, c2, 2, lambda: z_step(0, 2, flying))
     for copy in tables:
         copy.wait_recv()
     to_smem = pltpu.make_async_copy(tscr, tsm, lsem)
@@ -406,7 +405,7 @@
         x3[i] = jnp.where(low, c2[:, i], c2[i])
 
     each_row(build)
-    level(pm, x3, v3, g3, s3, c3, 4)
+    level(pm, x3, v3, g3, s3, c3, 4, lambda: None)
 
     def build(i):
         own = dd[i] - sroll(s3[i], 2)
@@ -507,20 +506,27 @@
         u3 = mvt(g3, rk3)
         own = ro + sroll(u3, 2)
         tip = ul + u2 + u3
-        v = jnp.where((slot == 1)[None], sroll(tip, 2), jnp.where((slot == 3)[None], own, 0.0))
-        v = exchange_groups(v)
-        for j in range(N):
-            vs[ph, pl.ds(j, 8, stride=VROWS), :] = v[j]
-        for j in range(N, VROWS):
-            vs[ph, pl.ds(j, 8, stride=VROWS), :] = jnp.zeros(tile, F32)
+        rows = []
+        for q in range(7):
+            j = 2 * q
+            v = jnp.where(slot == 0, tip[j], jnp.where(slot == 1, sroll(own[j], 4), 0.0))
+            if j + 1 < N:
+                v = jnp.where(slot == 2, sroll(tip[j + 1], 4), jnp.where(slot == 3, own[j + 1], v))
+            rows.append(v[None])
+        v = exchange_groups(jnp.concatenate(rows, axis=0))
+        for q in range(7):
+            vs[ph, pl.ds(q, 8, stride=VROWS), :] = v[q]
+        vs[ph, pl.ds(7, 8, stride=VROWS), :] = jnp.zeros(tile, F32)
         arriving = all_to_all(vs.at[ph], vr.at[ph], VROWS, vss.at[ph], vrs.at[ph])
         return re, rk2, rk3, arriving
 
     def separators(ph, arriving):
         for copy in arriving:
             copy.wait_recv()
-        got = jnp.concatenate([vr[ph, pl.ds(j, 8, stride=VROWS), :][None] for j in range(N)], axis=0)
-        r = lroll(got, 32) + jnp.where((sub < 7)[None], sroll(lroll(got, 96), -1), 0.0)
+        got = [vr[ph, pl.ds(q, 8, stride=VROWS), :] for q in range(7)]
+        tips = jnp.concatenate([(lroll(got[j // 2], 64) if j % 2 else got[j // 2])[None] for j in range(N)], axis=0)
+        owns = jnp.concatenate([lroll(got[j // 2], 32 if j % 2 else 96)[None] for j in range(N)], axis=0)
+        r = owns + jnp.where((sub < 7)[None], sroll(tips, -1), 0.0)
         even = (sub % 2 == 0)[None]
         fourth = (sub % 4 == 0)[None]
         rk1 = jnp.where(even, r, sroll(r, 1))
@@ -542,14 +548,14 @@
         u = mv(h1, near) + jnp.where(even, mvt(w1, rk1), 0.0)
         x = jnp.where(even, u + sroll(u, -1), x)
         below = jnp.where((sub == 0)[None], 0.0, sroll(x, 1))
-        quarter = (lane // 32)[None]
-        msg = jnp.where(
-            quarter == 0, below, jnp.where(quarter == 2, lroll(x, 64), jnp.where(quarter == 3, lroll(x, 96), 0.0))
-        )
-        for j in range(N):
-            bs[ph, pl.ds(j, 8, stride=VROWS), :] = msg[j]
-        for j in range(N, VROWS):
-            bs[ph, pl.ds(j, 8, stride=VROWS), :] = jnp.zeros(tile, F32)
+        quarter = lane // 32
+        for q in range(7):
+            j = 2 * q
+            v = jnp.where(quarter == 0, below[j], jnp.where(quarter == 1, lroll(x[j], 32), 0.0))
+            if j + 1 < N:
+                v = jnp.where(quarter == 2, lroll(below[j + 1], 64), jnp.where(quarter == 3, lroll(x[j + 1], 96), v))
+            bs[ph, pl.ds(q, 8, stride=VROWS), :] = v
+        bs[ph, pl.ds(7, 8, stride=VROWS), :] = jnp.zeros(tile, F32)
         return all_to_all(bs.at[ph], br.at[ph], VROWS, bss.at[ph], brs.at[ph])
 
     def backward(ph, kept, arriving):
@@ -557,8 +563,14 @@
         y1, y2, y3 = mvt(v1, re), mvt(v2, rk2), mvt(v3, rk3)
         for copy in arriving:
             copy.wait_recv()
-        got = jnp.concatenate([br[ph, pl.ds(j, 8, stride=VROWS), :][None] for j in range(N)], axis=0)
-        ends = exchange_groups(got)
+        got = jnp.concatenate([br[ph, pl.ds(q, 8, stride=VROWS), :][None] for q in range(7)], axis=0)
+        got = exchange_groups(got)
+        ends = []
+        for j in range(N):
+            v = got[j // 2]
+            low, mid, top = (sroll(v, 4), sroll(v, -2), v) if j % 2 else (v, sroll(v, 2), sroll(v, 4))
+            ends.append(jnp.where(slot == 0, low, jnp.where(slot == 2, mid, jnp.where(slot == 3, top, 0.0)))[None])
+        ends = jnp.concatenate(ends, axis=0)
         u = mv(g3, ends) + jnp.where((slot == 0)[None], y3, 0.0)
         x3 = sroll(u, 2) + sroll(u, -2)
         near = jnp.where((slot == 1)[None], x3, jnp.where((slot == 2)[None], sroll(x3, 2), ends))
@@ -634,16 +646,19 @@
     flying = {}
     z_step(1, 0, flying)
     inside(field)
-    for number in range(1, 5):
+    settle(4)
+    for number in (1, 2):
         z_step(1, number, flying)
     arriving = y_phase(1, flying)
+    settle(3)
     rhs = right_side(ghosts(1, arriving))
     kept = forward(1, rhs)
+    settle(7)
     back = separators(1, kept[3])
+    settle(7)
     out[...] = backward(1, kept, back)
 
-    for copy in sent:
-        copy.wait_send()
+    settle(0)
 
 
 def body(residual, previous, edge_blocks, damping, lateral, coupling, wall_flags, wall_gain, face_table):
@@ -689,8 +704,8 @@
             pltpu.VMEM((2, NLINE * VROWS, 128), F32),
             pltpu.VMEM((2, NLINE * VROWS, 128), F32),
             pltpu.VMEM((2, NLINE * VROWS, 128), F32),
-            dma((2, 2, 8)),
-            dma((2, 2, 8)),
+            dma((2, 3, 8)),
+            dma((2, 3, 8)),
             dma((2, NY - 1)),
             dma((2, NY - 1)),
             dma((NY - 1,)),

time: 75.8 us -> 73 us (0.963)
  Pallas kernels: 74 us -> 71.2 us
    pallas_call x1, Pallas kernels: 74 us -> 71.2 us  [body(): pl.pallas_call(kernel, out_shape=jax.ShapeDtypeStruct((N, 8, 256), F32),...]
where the time goes in v3:
time: 73 us; the launch traced here: 72.8 us
  Pallas kernels  71.2 us (98%)
  local copies, waits for them, and re-layouts  1.55 us (2%)
    pallas_call x1, Pallas kernels, body(): pl.pallas_call(kernel, out_shape=jax.ShapeDtypeStruct((N, 8, 256), F32),...  71.2 us
    unnamed x1, local copies, waits for them, and re-layouts  1.55 us

profile of v3, /device:TPU:1, one launch (start us, length us, event | category | flops | bytes accessed | tf_op | source)
XLA Modules:
  0.0 72.8 jit_solution(4614591058293341982)
XLA Ops:
  0.0 71.2 %line_sweeps.1 = f32[13,8,256]{2,1,0:T(8,128)} custom-call(f32[13,8,256]{2,1,0:T(8,128)} %bitcast.11, f32[13,8,256]{2,1,0:T(8,128)} %bitcast.12, bf16[13,13,8,256]{3,2,1,0:T(8,128)(2,1)} %bitcast.9, f32[13,8,256]{2,1,0:T(8,128)} %bitcast.13, f32[8,4,256]{2,1,0:T(4,128)} %lat_any.1, f32[13,13]{1,0:T(8,128)} %coup.1, s32[1,256]{1,0:T(1,128)} %bitcast.16, ...), custom_call_target="tpu_custom_call" | custom-call | tf_op jit(solution)/shard_map/line_sweeps/pallas_call | solution.py:673
  71.2 1.5 %copy.11 = f32[8,13,256]{2,0,1:T(8,128)} copy(f32[8,13,256]{2,0,1:T(8,128)} %bitcast.10) | data formatting | bytes 212992

commit v4 on v3

--- a/solution.py
+++ b/solution.py
@@ -238,8 +238,7 @@
 
     def z_step(ph, number, flying):
         waited, plan = (
-            (0, ((4, 4), (1, 1))),
-            (1, ((3, 2), (2, 1))),
+            (0, ((4, 4), (3, 3), (2, 2), (1, 1))),
             (4, ((8, 4), (7, 3), (6, 2), (5, 1))),
         )[number]
         if waited:
@@ -335,7 +334,6 @@
     inverse(pm, v1)
     mm(gl, v1, ue)
     mm(gr, v1, uo)
-    z_step(0, 1, flying)
     mm_upper(sl, ue, gl)
     mm_upper(sr, uo, gr)
     mm(c1, ue, gr)
@@ -391,7 +389,7 @@
         x2[i] = jnp.where(even, c1[:, i], c1[i])
 
     each_row(build)
-    level(pm, x2, v2, g2, s2, c2, 2, lambda: z_step(0, 2, flying))
+    level(pm, x2, v2, g2, s2, c2, 2, lambda: z_step(0, 1, flying))
     for copy in tables:
         copy.wait_recv()
     to_smem = pltpu.make_async_copy(tscr, tsm, lsem)
@@ -646,9 +644,8 @@
     flying = {}
     z_step(1, 0, flying)
     inside(field)
-    settle(4)
-    for number in (1, 2):
-        z_step(1, number, flying)
+    settle(8)
+    z_step(1, 1, flying)
     arriving = y_phase(1, flying)
     settle(3)
     rhs = right_side(ghosts(1, arriving))

time: 73 us -> 72.4 us (level)
  no operation moved by 1% of the time
where the time goes in v4:
time: 72.4 us; the launch traced here: 72.2 us
  Pallas kernels  70.6 us (98%)
  local copies, waits for them, and re-layouts  1.55 us (2%)
    pallas_call x1, Pallas kernels, body(): pl.pallas_call(kernel, out_shape=jax.ShapeDtypeStruct((N, 8, 256), F32),...  70.6 us
    unnamed x1, local copies, waits for them, and re-layouts  1.55 us

profile of v4, /device:TPU:1, one launch (start us, length us, event | category | flops | bytes accessed | tf_op | source)
XLA Modules:
  0.0 72.2 jit_solution(9436223088829199899)
XLA Ops:
  0.0 70.6 %line_sweeps.1 = f32[13,8,256]{2,1,0:T(8,128)} custom-call(f32[13,8,256]{2,1,0:T(8,128)} %bitcast.11, f32[13,8,256]{2,1,0:T(8,128)} %bitcast.12, bf16[13,13,8,256]{3,2,1,0:T(8,128)(2,1)} %bitcast.9, f32[13,8,256]{2,1,0:T(8,128)} %bitcast.13, f32[8,4,256]{2,1,0:T(4,128)} %lat_any.1, f32[13,13]{1,0:T(8,128)} %coup.1, s32[1,256]{1,0:T(1,128)} %bitcast.16, ...), custom_call_target="tpu_custom_call" | custom-call | tf_op jit(solution)/shard_map/line_sweeps/pallas_call | solution.py:670
  70.6 1.5 %copy.11 = f32[8,13,256]{2,0,1:T(8,128)} copy(f32[8,13,256]{2,0,1:T(8,128)} %bitcast.10) | data formatting | bytes 212992
